TPU v7x, 512 devices: a whole 4x8x8 slice. The times are simulated.
512 devices in a mesh: dp: 32 (over x, y), seq: 16 (over z, core).
Axes of the slice: x: 4, y: 8, z: 8, core: 2. Of those that a mesh axis runs over, the one named last changes fastest.
Arguments:
- volume: bfloat16 [32, 3072, 1024], P('dp', 'seq')
- cotangent: bfloat16 [32, 3072, 1024], P('dp', 'seq'), may hold values from -6 to 6
- weights: bfloat16 [1024, 3, 1024], P('dp')
- pairs: int32 [32, 16, 24, 4], P('dp', 'seq'), may hold values from 0 to 23, as said below
- valid: int32 [32, 16, 24, 4], P('dp', 'seq'), may hold values from 0 to 1, as said below
Outputs:
- attended: bfloat16 [32, 3072, 1024], P('dp', 'seq')
- weight_grad: float32 [1024, 3, 1024], P('dp', None, 'seq')
Inputs may be any that keep to these rules, and one draw needn't show every extreme that they name: `pairs`: slot 0 of query block b holds b; the key blocks of one query block's slots are distinct. `valid`: slot 0 is always 1.
All inputs are finite; a program needn't handle non-finite values.
Results may differ from a plain program's by a relative error of at most 0.03.
Values may be sent and summed in bfloat16 or wider, within the bound.
No kernel may reach another device: no remote copies, remote signals or barrier semaphores. Data moves between devices by JAX's collectives and lax.ppermute only.
A program may use at most 64 MiB of HBM per device.

v0:
```python
import math
import jax
import jax.numpy as jnp
from jax import lax
from jax.sharding import PartitionSpec as P

HD = 64


def head_pass(queries, keys_all, values_all, upstream, pair_list, pair_live):
    block_count, slot_count = pair_list.shape
    all_rows, head_size = queries.shape
    block_rows = all_rows // block_count
    per_step = math.gcd(block_count, max(1, 512 // block_rows))
    steps_n = block_count // per_step
    scaling = head_size ** (-0.5)
    key_blocks = keys_all.reshape(block_count, block_rows, head_size)
    value_blocks = values_all.reshape(block_count, block_rows, head_size)
    block_index = jnp.arange(block_count, dtype=jnp.int32)

    def step(totals, sliced):
        key_total, value_total = totals
        query_rows, grad_rows, slot_blocks, slot_live = sliced
        key_rows = key_blocks[slot_blocks].reshape(per_step, slot_count * block_rows, head_size)
        value_rows = value_blocks[slot_blocks].reshape(per_step, slot_count * block_rows, head_size)
        live_cols = jnp.repeat(slot_live > 0, block_rows, axis=1)[:, None, :]
        scores = (
            jnp.einsum("nqd,nkd->nqk", query_rows, key_rows, preferred_element_type=jnp.float32)
            * scaling
        )
        row_max = jnp.max(jnp.where(live_cols, scores, -1e30), axis=-1, keepdims=True)
        exponent = jnp.where(live_cols, jnp.exp(scores - row_max), 0.0)
        prob_full = exponent / jnp.sum(exponent, axis=-1, keepdims=True)
        rounded = prob_full.astype(jnp.bfloat16)
        result = jnp.einsum(
            "nqk,nkd->nqd", rounded, value_rows, preferred_element_type=jnp.float32
        ).astype(jnp.bfloat16)
        value_grad = jnp.einsum(
            "nqk,nqd->nkd", rounded, grad_rows, preferred_element_type=jnp.float32
        )
        prob_grad = jnp.einsum(
            "nqd,nkd->nqk", grad_rows, value_rows, preferred_element_type=jnp.float32
        )
        row_dot = jnp.sum(
            grad_rows.astype(jnp.float32) * result.astype(jnp.float32), axis=-1, keepdims=True
        )
        score_grad = (prob_full * (prob_grad - row_dot) * scaling).astype(jnp.bfloat16)
        query_grad = jnp.einsum(
            "nqk,nkd->nqd", score_grad, key_rows, preferred_element_type=jnp.float32
        ).astype(jnp.bfloat16)
        key_grad = jnp.einsum(
            "nqk,nqd->nkd", score_grad, query_rows, preferred_element_type=jnp.float32
        )
        one_hot = (
            (slot_blocks.reshape(-1)[:, None] == block_index[None, :])
            & (slot_live.reshape(-1)[:, None] > 0)
        ).astype(jnp.float32)
        key_total = key_total + jnp.einsum(
            "jb,jrd->brd",
            one_hot,
            key_grad.reshape(per_step * slot_count, block_rows, head_size),
            precision=lax.Precision.HIGHEST,
        )
        value_total = value_total + jnp.einsum(
            "jb,jrd->brd",
            one_hot,
            value_grad.reshape(per_step * slot_count, block_rows, head_size),
            precision=lax.Precision.HIGHEST,
        )
        return ((key_total, value_total), (result, query_grad))

    empty_acc = jnp.zeros((block_count, block_rows, head_size), jnp.float32)
    sliced_all = (
        queries.reshape(steps_n, per_step, block_rows, head_size),
        upstream.reshape(steps_n, per_step, block_rows, head_size),
        pair_list.reshape(steps_n, per_step, slot_count),
        pair_live.reshape(steps_n, per_step, slot_count),
    )
    (key_total, value_total), (results, query_grads) = lax.scan(
        step, (empty_acc, empty_acc), sliced_all
    )
    return (
        results.reshape(all_rows, head_size),
        query_grads.reshape(all_rows, head_size),
        key_total.astype(jnp.bfloat16).reshape(all_rows, head_size),
        value_total.astype(jnp.bfloat16).reshape(all_rows, head_size),
    )


def local(volume, cotangent, weights, pairs, valid):
    seq_devices = lax.axis_size("seq")
    local_volume = volume[0]
    local_grad = cotangent[0]
    tok_count = local_volume.shape[0]
    width_all = local_grad.shape[1]
    local_cols = width_all // seq_devices
    all_rows = tok_count * seq_devices
    projected = jnp.einsum(
        "td,djc->tjc",
        local_volume,
        lax.all_gather(weights, "dp", axis=0, tiled=True),
        preferred_element_type=jnp.float32,
    )
    projected = projected.astype(jnp.bfloat16)
    head_inputs, head_grad = (
        lax.all_to_all(projected, "seq", split_axis=2, concat_axis=0, tiled=True),
        lax.all_to_all(
            local_grad.reshape(tok_count, 1, width_all),
            "seq",
            split_axis=2,
            concat_axis=0,
            tiled=True,
        ),
    )
    head_grad = head_grad.reshape(all_rows, local_cols)
    upper = HD
    result, query_grad, key_grad, value_grad = head_pass(
        head_inputs[:, 0, 0:upper],
        head_inputs[:, 1, 0:upper],
        head_inputs[:, 2, 0:upper],
        head_grad,
        pairs[0, 0],
        valid[0, 0],
    )
    grad_flat = jnp.stack([query_grad, key_grad, value_grad], axis=1).reshape(
        all_rows, 3 * local_cols
    )
    attended = lax.all_to_all(result, "seq", split_axis=0, concat_axis=1, tiled=True)
    local_sum = lax.dot_general(
        lax.all_gather(local_volume, "seq", axis=0, tiled=True),
        grad_flat,
        (((0,), (0,)), ((), ())),
        preferred_element_type=jnp.float32,
    )
    weight_part = (
        lax.psum_scatter(local_sum.astype(jnp.bfloat16), "dp", scatter_dimension=0, tiled=True)
        .astype(jnp.float32)
        .reshape(-1, 3, local_cols)
    )
    return (attended[None], weight_part)


def solution(mesh):
    return jax.shard_map(
        local,
        mesh=mesh,
        in_specs=(
            P("dp", "seq", None),
            P("dp", "seq", None),
            P("dp", None, None),
            P("dp", "seq", None, None),
            P("dp", "seq", None, None),
        ),
        out_specs=(P("dp", "seq", None), P("dp", None, "seq")),
        check_vma=False,
    )
```

profile of v0, /device:TPU:16, one launch (start us, length us, event | category | flops | bytes accessed | tf_op | source)
XLA Modules:
  0.0 509.1 jit_solution(6228003603930186872)
XLA Ops:
  8.7 2.4 copy.66
  11.6 4.1 reduce
  17.1 10.4 %all-to-all-start.1 = ((bf16[16,2,6144]{2,1,0:T(2,128)(2,1)}), bf16[16,2,6144]{2,1,0:T(2,128)(2,1)S(1)}, u32[]{:S(2)}, u32[]{:S(2)}) async-start(bf16[16,2,6144]{2,1,0:T(2,128)(2,1)} %reshape.121), calls=%async_computation.1 | async-start | bytes 786432 | tf_op jit(solution)/shard_map/all_to_all | solution.py:107
  27.5 81.9 %all-gather.4.cloned.1.call-done = bf16[1024,3,1024]{2,0,1:T(8,128)(2,1)} async-done(((bf16[32,3,1024]{2,0,1:T(8,128)(2,1)}), bf16[1024,3,1024]{2,0,1:T(8,128)(2,1)}) %all-gather.4.cloned.1.call-update) | async-done | bytes 6291472 | tf_op jit(solution)/shard_map/all_gather | solution.py:101
  109.4 4.2 convolution_convert_fusion.2
  113.6 2.6 copy.63
  116.2 7.6 %all-to-all-start = ((bf16[192,3,1024]{0,1,2:T(4,128)(2,1)}), bf16[192,3,1024]{0,1,2:T(4,128)(2,1)S(1)}, u32[]{:S(2)}, u32[]{:S(2)}) async-start(bf16[192,3,1024]{0,1,2:T(4,128)(2,1)} %copy.63), calls=%async_computation | async-start | bytes 4194304 | tf_op jit(solution)/shard_map/all_to_all | solution.py:106
  125.4 2.0 reshape.122
  130.4 57.3 %all-to-all-done = bf16[192,3,1024]{0,1,2:T(4,128)(2,1)S(1)} async-done(((bf16[192,3,1024]{0,1,2:T(4,128)(2,1)}), bf16[192,3,1024]{0,1,2:T(4,128)(2,1)S(1)}, u32[]{:S(2)}, u32[]{:S(2)}) %all-to-all-start) | async-done | bytes 1179680 | tf_op jit(solution)/shard_map/all_to_all | solution.py:106
  194.0 83.2 %while.17 = (s32[]{:T(128)}, f32[24,128,64]{1,0,2:T(8,128)S(1)}, f32[24,128,64]{1,0,2:T(8,128)}, bf16[6,4,128,64]{2,1,0,3:T(4,128)(2,1)}, bf16[6,4,128,64]{2,1,0...) while((s32[]{:T(128)}, f32[24,128,64]{1,0,2:T(8,128)S(1)}, ...), condition=%wide.region_4.5_spmd.clone, body=%wide.region_0.4_spmd.clone.sunk | while | flops 280955456 | bytes 27224828 | solution.py:79
  194.7 1.8 gather_fusion.1
  198.9 1.8 gather_fusion
  208.7 1.8 gather_fusion.1
  212.8 1.8 gather_fusion
  222.5 1.8 gather_fusion.1
  226.7 1.8 gather_fusion
  236.4 1.8 gather_fusion.1
  240.5 1.8 gather_fusion
  250.2 1.8 gather_fusion.1
  254.4 1.8 gather_fusion
  268.2 1.8 gather_fusion
  279.0 4.2 fusion.34
  284.8 23.0 %all_to_all.49 = bf16[16,192,64]{1,2,0:T(8,128)(2,1)S(1)} all-to-all(bf16[16,192,64]{1,2,0:T(8,128)(2,1)S(1)} %copy.75), channel_id=1, replica_groups=mesh['dp'=32,'seq'=16] {'seq'}, dimensions={0} | all-to-all | bytes 786432 | tf_op jit(solution)/shard_map/all_to_all | solution.py:128
  308.7 191.4 %reduce-scatter.4.cloned.1.call-done = bf16[32,192]{1,0:T(8,128)(2,1)} async-done(((bf16[1024,192]{1,0:T(8,128)(2,1)}), bf16[32,192]{1,0:T(8,128)(2,1)}) %reduce-scatter.4.cloned.1.call-update) | async-done | bytes 12304
  (255 shorter events, 81.9 us)
Async XLA Ops:
  8.0 101.4 %all-gather.4.cloned.1.call-start = ((), (), s32[]{:S(2)}) async-start(), calls=%async_computation.4 | async-start | bytes 6488064 | tf_op jit(solution)/shard_map/all_gather | solution.py:101
  11.6 97.8 %copy-start.3 = (bf16[1,192,1024]{2,1,0:T(8,128)(2,1)S(1)}, bf16[1,192,1024]{2,1,0:T(8,128)(2,1)}, u32[]{:S(2)}) copy-start(bf16[1,192,1024]{2,1,0:T(8,128)(2,1)} %param.7) | copy-start | bytes 1179652
  17.1 99.1 %all-to-all-start.1 = ((bf16[16,2,6144]{2,1,0:T(2,128)(2,1)}), bf16[16,2,6144]{2,1,0:T(2,128)(2,1)S(1)}, u32[]{:S(2)}, u32[]{:S(2)}) async-start(bf16[16,2,6144]{2,1,0:T(2,128)(2,1)} %reshape.121), calls=%async_computation.1 | async-start | bytes 786432 | tf_op jit(solution)/shard_map/all_to_all | solution.py:107
  116.2 8.5 %copy-start.8 = (s32[1,1,24,4]{2,3,1,0:T(4,128)S(1)}, s32[1,1,24,4]{2,3,1,0:T(4,128)}, u32[]{:S(2)}) copy-start(s32[1,1,24,4]{2,3,1,0:T(4,128)} %param.10) | copy-start | bytes 1156
  116.2 9.2 %copy-start.9 = (s32[1,1,24,4]{2,3,1,0:T(4,128)S(1)}, s32[1,1,24,4]{2,3,1,0:T(4,128)}, u32[]{:S(2)}) copy-start(s32[1,1,24,4]{2,3,1,0:T(4,128)} %param.11) | copy-start | bytes 1156
  116.2 71.5 %all-to-all-start = ((bf16[192,3,1024]{0,1,2:T(4,128)(2,1)}), bf16[192,3,1024]{0,1,2:T(4,128)(2,1)S(1)}, u32[]{:S(2)}, u32[]{:S(2)}) async-start(bf16[192,3,1024]{0,1,2:T(4,128)(2,1)} %copy.63), calls=%async_computation | async-start | bytes 4194304 | tf_op jit(solution)/shard_map/all_to_all | solution.py:106
  123.8 155.2 %all-gather.6.cloned.1.call-start = ((), (), s32[]{:S(2)}) async-start(), calls=%async_computation.5 | async-start | bytes 6684672 | tf_op jit(solution)/shard_map/all_gather | solution.py:130
  124.4 375.7 %reduce-scatter.4.cloned.1.call-start = ((), (), s32[]{:S(2)}) async-start(), calls=%async_computation.6 | async-start | bytes 540672
  194.0 4.0 copy-start.6
  205.1 1.1 copy-start
  207.9 3.9 copy-start.6
  219.0 1.1 copy-start
  220.8 0.9 copy-start.1
  221.7 3.9 copy-start.6
  232.8 1.1 copy-start
  235.6 3.9 copy-start.6
  246.7 1.1 copy-start
  249.4 3.9 copy-start.6
  260.6 1.1 copy-start
  263.3 3.9 copy-start.6
  274.4 1.1 copy-start
  277.2 1.1 copy-start.2
  277.2 1.3 copy-start.5
  283.2 1.0 copy-start.4
  (11 other events, 9.7 us)
Sparse Core Ops, SparseCore 0:
  12.0 97.3 all-gather.3
  284.4 215.6 reduce-scatter.3
Sparse Core Ops, SparseCore 1:
  126.4 77.8 all-gather.5
where the time goes:
time: 511 us; the launch traced here: 509 us
  waiting for transfers between devices  332 us (65%)
  local copies, waits for them, and re-layouts  76.9 us (15%)
  matrix products  27.8 us (5%)
  blocking collectives  23 us (5%)
  starting transfers between devices  18.3 us (4%)
  between operations  15.7 us (3%)
  other arithmetic  14.6 us (3%)
    unnamed x4, waiting for transfers between devices  193 us
    all_gather x1, waiting for transfers between devices, local(): lax.all_gather(weights, 'dp', axis=0, tiled=True)  81.9 us
    all_to_all x1, waiting for transfers between devices, local(): lax.all_to_all(projected, 'seq', split_axis=2, concat_axis=0, tiled=True)  57.3 us
    all_to_all x1, blocking collectives, local(): lax.all_to_all(result, 'seq', split_axis=0, concat_axis=1, tiled=True)  23 us
    unnamed x24, local copies, waits for them, and re-layouts  12.6 us
    gather x6, local copies, waits for them, and re-layouts, step(): key_blocks[slot_blocks]  10.7 us
    gather x6, local copies, waits for them, and re-layouts, step(): value_blocks[slot_blocks]  10.7 us
    dynamic_slice x12, local copies, waits for them, and re-layouts, head_pass(): lax.scan(step, (empty_acc, empty_acc), sliced_all)  10.5 us
  transfers between devices with their start and end apart: 5, of which 3 were waited for; matrix products, arithmetic and copies ran while one was open for 20% of the time, Pallas kernels for 0%

commit v1 on v0

--- a/solution.py
+++ b/solution.py
@@ -125,7 +125,12 @@
     grad_flat = jnp.stack([query_grad, key_grad, value_grad], axis=1).reshape(
         all_rows, 3 * local_cols
     )
-    attended = lax.all_to_all(result, "seq", split_axis=0, concat_axis=1, tiled=True)
+    attended = jnp.concatenate(
+        jax.lax.all_to_all(
+            jnp.stack(jnp.split(result, jax.lax.axis_size("seq"), axis=0)), "seq", 0, 0
+        ),
+        axis=1,
+    )
     local_sum = lax.dot_general(
         lax.all_gather(local_volume, "seq", axis=0, tiled=True),
         grad_flat,

time: 511 us -> 522 us (1.022)
  local copies, waits for them, and re-layouts: 76.9 us -> 87.6 us
    unnamed x24 -> x37, local copies, waits for them, and re-layouts: 12.6 us -> 21.9 us
  transfers between devices with their start and end apart: 5 -> 5, of which waited for: 3 -> 3; matrix products, arithmetic and copies ran while one was open for 20% -> 22% of each run, Pallas kernels for 0% -> 0%
where the time goes in v1:
time: 522 us; the launch traced here: 519 us
  waiting for transfers between devices  331 us (63%)
  local copies, waits for them, and re-layouts  87.6 us (17%)
  matrix products  27.8 us (5%)
  blocking collectives  23.2 us (4%)
  starting transfers between devices  18.3 us (4%)
  between operations  15.7 us (3%)
  other arithmetic  14.6 us (3%)
    unnamed x4, waiting for transfers between devices  192 us
    all_gather x1, waiting for transfers between devices, local(): lax.all_gather(weights, 'dp', axis=0, tiled=True)  81.9 us
    all_to_all x1, waiting for transfers between devices, local(): lax.all_to_all(projected, 'seq', split_axis=2, concat_axis=0, tiled=True)  57.2 us
    all_to_all x1, blocking collectives, local(): jax.lax.all_to_all(jnp.stack(jnp.split(result, jax.lax.axis_size('seq'),...  23.2 us
    unnamed x37, local copies, waits for them, and re-layouts  21.9 us
    gather x6, local copies, waits for them, and re-layouts, step(): key_blocks[slot_blocks]  10.7 us
    gather x6, local copies, waits for them, and re-layouts, step(): value_blocks[slot_blocks]  10.7 us
    dynamic_slice x12, local copies, waits for them, and re-layouts, head_pass(): lax.scan(step, (empty_acc, empty_acc), sliced_all)  10.5 us
  transfers between devices with their start and end apart: 5, of which 3 were waited for; matrix products, arithmetic and copies ran while one was open for 22% of the time, Pallas kernels for 0%

profile of v1, /device:TPU:16, one launch (start us, length us, event | category | flops | bytes accessed | tf_op | source)
XLA Modules:
  0.0 519.4 jit_solution(10510475183071606123)
XLA Ops:
  8.7 2.4 copy.79
  11.6 4.1 reduce
  17.1 10.4 %all-to-all-start.1 = ((bf16[16,2,6144]{2,1,0:T(2,128)(2,1)}), bf16[16,2,6144]{2,1,0:T(2,128)(2,1)S(1)}, u32[]{:S(2)}, u32[]{:S(2)}) async-start(bf16[16,2,6144]{2,1,0:T(2,128)(2,1)} %reshape.123), calls=%async_computation.1 | async-start | bytes 786432 | tf_op jit(solution)/shard_map/all_to_all | solution.py:107
  27.5 81.9 %all-gather.4.cloned.1.call-done = bf16[1024,3,1024]{2,0,1:T(8,128)(2,1)} async-done(((bf16[32,3,1024]{2,0,1:T(8,128)(2,1)}), bf16[1024,3,1024]{2,0,1:T(8,128)(2,1)}) %all-gather.4.cloned.1.call-update) | async-done | bytes 6291472 | tf_op jit(solution)/shard_map/all_gather | solution.py:101
  109.4 4.2 convolution_convert_fusion.2
  113.6 2.6 copy.76
  116.2 7.6 %all-to-all-start = ((bf16[192,3,1024]{0,1,2:T(4,128)(2,1)}), bf16[192,3,1024]{0,1,2:T(4,128)(2,1)S(1)}, u32[]{:S(2)}, u32[]{:S(2)}) async-start(bf16[192,3,1024]{0,1,2:T(4,128)(2,1)} %copy.76), calls=%async_computation | async-start | bytes 4194304 | tf_op jit(solution)/shard_map/all_to_all | solution.py:106
  125.4 2.0 reshape.124
  130.4 57.2 %all-to-all-done = bf16[192,3,1024]{0,1,2:T(4,128)(2,1)S(1)} async-done(((bf16[192,3,1024]{0,1,2:T(4,128)(2,1)}), bf16[192,3,1024]{0,1,2:T(4,128)(2,1)S(1)}, u32[]{:S(2)}, u32[]{:S(2)}) %all-to-all-start) | async-done | bytes 1179680 | tf_op jit(solution)/shard_map/all_to_all | solution.py:106
  194.0 83.1 %while.17 = (s32[]{:T(128)}, f32[24,128,64]{1,0,2:T(8,128)S(1)}, f32[24,128,64]{1,0,2:T(8,128)}, bf16[6,4,128,64]{2,1,0,3:T(4,128)(2,1)}, bf16[6,4,128,64]{2,1,0...) while((s32[]{:T(128)}, f32[24,128,64]{1,0,2:T(8,128)S(1)}, ...), condition=%wide.region_4.5_spmd.clone, body=%wide.region_0.4_spmd.clone.sunk | while | flops 280955456 | bytes 27224828 | solution.py:79
  194.7 1.8 gather_fusion.1
  198.9 1.8 gather_fusion
  208.6 1.8 gather_fusion.1
  212.8 1.8 gather_fusion
  222.5 1.8 gather_fusion.1
  226.6 1.8 gather_fusion
  236.3 1.8 gather_fusion.1
  240.5 1.8 gather_fusion
  250.2 1.8 gather_fusion.1
  254.3 1.8 gather_fusion
  268.2 1.8 gather_fusion
  289.6 4.2 fusion.34
  295.5 23.2 %all_to_all.38 = bf16[16,192,64]{1,2,0:T(8,128)(2,1)S(1)} all-to-all(bf16[16,192,64]{1,2,0:T(8,128)(2,1)} %constant_dynamic-update-slice_fusion), channel_id=1, replica_groups=mesh['dp'=32,'seq'=16] {'seq'}, dimensions={0} | all-to-all | bytes 786432 | tf_op jit(solution)/shard_map/all_to_all | solution.py:129
  319.6 190.7 %reduce-scatter.4.cloned.1.call-done = bf16[32,192]{1,0:T(8,128)(2,1)} async-done(((bf16[1024,192]{1,0:T(8,128)(2,1)}), bf16[32,192]{1,0:T(8,128)(2,1)}) %reduce-scatter.4.cloned.1.call-update) | async-done | bytes 12304
  (268 shorter events, 92.6 us)
Async XLA Ops:
  8.0 101.4 %all-gather.4.cloned.1.call-start = ((), (), s32[]{:S(2)}) async-start(), calls=%async_computation.4 | async-start | bytes 6488064 | tf_op jit(solution)/shard_map/all_gather | solution.py:101
  11.6 97.8 %copy-start.3 = (bf16[1,192,1024]{2,1,0:T(8,128)(2,1)S(1)}, bf16[1,192,1024]{2,1,0:T(8,128)(2,1)}, u32[]{:S(2)}) copy-start(bf16[1,192,1024]{2,1,0:T(8,128)(2,1)} %param.7) | copy-start | bytes 1179652
  17.1 99.1 %all-to-all-start.1 = ((bf16[16,2,6144]{2,1,0:T(2,128)(2,1)}), bf16[16,2,6144]{2,1,0:T(2,128)(2,1)S(1)}, u32[]{:S(2)}, u32[]{:S(2)}) async-start(bf16[16,2,6144]{2,1,0:T(2,128)(2,1)} %reshape.123), calls=%async_computation.1 | async-start | bytes 786432 | tf_op jit(solution)/shard_map/all_to_all | solution.py:107
  116.2 8.5 %copy-start.7 = (s32[1,1,24,4]{2,3,1,0:T(4,128)S(1)}, s32[1,1,24,4]{2,3,1,0:T(4,128)}, u32[]{:S(2)}) copy-start(s32[1,1,24,4]{2,3,1,0:T(4,128)} %param.10) | copy-start | bytes 1156
  116.2 9.2 %copy-start.8 = (s32[1,1,24,4]{2,3,1,0:T(4,128)S(1)}, s32[1,1,24,4]{2,3,1,0:T(4,128)}, u32[]{:S(2)}) copy-start(s32[1,1,24,4]{2,3,1,0:T(4,128)} %param.11) | copy-start | bytes 1156
  116.2 71.5 %all-to-all-start = ((bf16[192,3,1024]{0,1,2:T(4,128)(2,1)}), bf16[192,3,1024]{0,1,2:T(4,128)(2,1)S(1)}, u32[]{:S(2)}, u32[]{:S(2)}) async-start(bf16[192,3,1024]{0,1,2:T(4,128)(2,1)} %copy.76), calls=%async_computation | async-start | bytes 4194304 | tf_op jit(solution)/shard_map/all_to_all | solution.py:106
  123.8 165.8 %all-gather.6.cloned.1.call-start = ((), (), s32[]{:S(2)}) async-start(), calls=%async_computation.5 | async-start | bytes 6684672 | tf_op jit(solution)/shard_map/all_gather | solution.py:135
  124.4 386.0 %reduce-scatter.4.cloned.1.call-start = ((), (), s32[]{:S(2)}) async-start(), calls=%async_computation.6 | async-start | bytes 540672
  194.0 4.0 copy-start.5
  205.1 1.1 copy-start
  207.0 0.9 copy-start.1
  207.8 3.9 copy-start.5
  219.0 1.1 copy-start
  221.7 3.9 copy-start.5
  232.8 1.1 copy-start
  234.7 0.9 copy-start.1
  235.6 3.9 copy-start.5
  246.7 1.1 copy-start
  249.4 3.9 copy-start.5
  260.5 1.1 copy-start
  263.3 3.9 copy-start.5
  274.4 1.1 copy-start
  277.1 1.6 copy-start.2
  278.5 1.0 copy-start.4
  (10 other events, 8.8 us)
Sparse Core Ops, SparseCore 0:
  12.0 97.3 all-gather.3
  294.9 215.3 reduce-scatter.3
Sparse Core Ops, SparseCore 1:
  126.4 77.8 all-gather.5
